TPU v7x, 1024 devices: a whole 8x8x8 slice. The times are simulated.
1024 devices in a mesh: row: 16 (over z, core), col: 64 (over y, x).
Axes of the slice: x: 8, y: 8, z: 8, core: 2. Of those that a mesh axis runs over, the one named last changes fastest.
Arguments:
- users: bfloat16 [16, 64, 32, 128], P('row', 'col'), may hold values from -6 to 6
- items: bfloat16 [64, 16, 128, 128], P('col', 'row'), may hold values from -6 to 6
- user_degree: int32 [16, 64, 32], P('row', 'col'), may hold values from 1 to 16
- item_degree: int32 [64, 16, 128], P('col', 'row'), may hold values from 1 to 16
- tile_values: bfloat16 [16, 64, 48, 128, 128], P('row', 'col'), may hold values from -0.25 to 0.25
- tile_rows: int32 [16, 64, 48], P('row', 'col'), may hold values from 0 to 15
- tile_cols: int32 [16, 64, 48], P('row', 'col'), may hold values from 0 to 15
- tile_count: int32 [16, 64], P('row', 'col'), may hold values from 16 to 48, as said below
- bpr_user: int32 [16, 64, 256], P('row', 'col'), may hold values from 0 to 31
- bpr_pos: int32 [16, 64, 256], P('row', 'col'), may hold values from 0 to 127
- bpr_neg: int32 [16, 64, 256], P('row', 'col'), may hold values from 0 to 127
Outputs:
- user_out: bfloat16 [16, 64, 32, 128], P('row', 'col')
- item_out: bfloat16 [64, 16, 128, 128], P('col', 'row')
- grad_users: float32 [16, 64, 32, 128], P('row', 'col')
- grad_items: float32 [64, 16, 128, 128], P('col', 'row')
Inputs may be any that keep to these rules, and one draw needn't show every extreme that they name: `tile_count`: at least a third of the slots are live on every device, and some device has all 48 slots live.
All inputs are finite; a program needn't handle non-finite values.
Results may differ from a plain program's by a relative error of at most 0.0069.
Values may be sent and summed in bfloat16 or wider, within the bound.
A program may use at most 32 MiB of HBM per device.

v0:
```python
import jax
import jax.numpy as jnp
from jax import lax
from jax.sharding import PartitionSpec as P


def propagate(user_in, item_in, user_scale, item_scale, tiles, rows, cols, live):
    width = user_in.shape[3]
    user_cnt = user_in.shape[2]
    item_cnt = item_in.shape[2]
    ncol = lax.axis_size("col")
    nrow = lax.axis_size("row")
    tile_side = tiles.shape[1]
    scaled_users = (user_in.astype(jnp.float32) * user_scale).astype(jnp.bfloat16)
    scaled_items = (item_in.astype(jnp.float32) * item_scale).astype(jnp.bfloat16)
    user_region = lax.all_gather(scaled_users, "col", axis=1, tiled=True).reshape(
        -1, tile_side, width
    )
    item_region = lax.all_gather(scaled_items, "row", axis=1, tiled=True).reshape(
        -1, tile_side, width
    )
    item_blocks = jnp.take(item_region, cols, axis=0)
    user_blocks = jnp.take(user_region, rows, axis=0)
    to_users = jnp.einsum("sab,sbd->sad", tiles, item_blocks, preferred_element_type=jnp.float32)
    to_items = jnp.einsum("sab,sad->sbd", tiles, user_blocks, preferred_element_type=jnp.float32)
    hot_rows = (
        (rows[None, :] == jnp.arange(user_region.shape[0])[:, None]) & live[None, :]
    ).astype(jnp.float32)
    hot_cols = (
        (cols[None, :] == jnp.arange(item_region.shape[0])[:, None]) & live[None, :]
    ).astype(jnp.float32)
    user_part = jnp.einsum("ts,sad->tad", hot_rows, to_users, precision=lax.Precision.HIGHEST)
    item_part = jnp.einsum("ts,sad->tad", hot_cols, to_items, precision=lax.Precision.HIGHEST)
    user_sum = lax.psum_scatter(
        user_part.reshape(1, ncol, user_cnt, width), "col", scatter_dimension=1, tiled=True
    )
    item_sum = lax.psum_scatter(
        item_part.reshape(1, nrow, item_cnt, width), "row", scatter_dimension=1, tiled=True
    )
    return (user_sum * user_scale, item_sum * item_scale)


def triple_grads(user_local, item_local, who, positive, negative):
    hot_user = (who[:, None] == jnp.arange(user_local.shape[0])[None, :]).astype(jnp.float32)
    hot_pos = (positive[:, None] == jnp.arange(item_local.shape[0])[None, :]).astype(jnp.float32)
    hot_neg = (negative[:, None] == jnp.arange(item_local.shape[0])[None, :]).astype(jnp.float32)
    highest = lax.Precision.HIGHEST
    user_vec = jnp.dot(hot_user, user_local, precision=highest)
    pos_vec = jnp.dot(hot_pos, item_local, precision=highest)
    neg_vec = jnp.dot(hot_neg, item_local, precision=highest)
    score = jnp.sum(user_vec * (pos_vec - neg_vec), axis=1)
    weight = jax.nn.sigmoid(-score)[:, None]
    grad_u = jnp.dot(hot_user.T, -weight * (pos_vec - neg_vec), precision=highest)
    grad_i = jnp.dot(hot_pos.T, -weight * user_vec, precision=highest) + jnp.dot(
        hot_neg.T, weight * user_vec, precision=highest
    )
    return (grad_u, grad_i)


def local(
    users,
    items,
    user_degree,
    item_degree,
    tile_values,
    tile_rows,
    tile_cols,
    tile_count,
    bpr_user,
    bpr_pos,
    bpr_neg,
):
    user_scale = lax.rsqrt(user_degree.astype(jnp.float32))[..., None]
    item_scale = lax.rsqrt(item_degree.astype(jnp.float32))[..., None]
    tiles = tile_values[0, 0]
    rows = tile_rows[0, 0]
    cols = tile_cols[0, 0]
    live = jnp.arange(tiles.shape[0]) < tile_count[0, 0]
    user_res, item_res = propagate(users, items, user_scale, item_scale, tiles, rows, cols, live)
    user_out = user_res.astype(jnp.bfloat16)
    item_out = item_res.astype(jnp.bfloat16)
    grad_u, grad_i = triple_grads(
        user_out[0, 0].astype(jnp.float32),
        item_out[0, 0].astype(jnp.float32),
        bpr_user[0, 0],
        bpr_pos[0, 0],
        bpr_neg[0, 0],
    )
    grad_users, grad_items = propagate(
        grad_u[None, None], grad_i[None, None], user_scale, item_scale, tiles, rows, cols, live
    )
    return (user_out, item_out, grad_users, grad_items)


def solution(mesh):
    return jax.shard_map(
        local,
        mesh=mesh,
        in_specs=(
            P("row", "col", None, None),
            P("col", "row", None, None),
            P("row", "col", None),
            P("col", "row", None),
            P("row", "col", None, None, None),
            P("row", "col", None),
            P("row", "col", None),
            P("row", "col"),
            P("row", "col", None),
            P("row", "col", None),
            P("row", "col", None),
        ),
        out_specs=(
            P("row", "col", None, None),
            P("col", "row", None, None),
            P("row", "col", None, None),
            P("col", "row", None, None),
        ),
        check_vma=False,
    )
```

profile of v0, /device:TPU:1, one launch (start us, length us, event | category | flops | bytes accessed | tf_op | source)
XLA Modules:
  0.0 778.0 jit_solution(12102893612052617153)
XLA Ops:
  10.1 40.3 %all_gather.13 = bf16[1,64,32,128]{3,2,0,1:T(8,128)(2,1)S(1)} all-gather(bf16[1,1,32,128]{3,2,0,1:T(8,128)(2,1)S(1)} %fusion.44), channel_id=1, replica_groups=mesh['row'=16,'col'=64] {'col'}, dimensions={1}, use_global_device_ids=true | all-gather | bytes 532480 | tf_op jit(solution)/shard_map/all_gather | solution.py:16
  50.4 2.0 gather_fusion.1
  52.3 3.8 convolution_bitcast_fusion.2
  56.1 3.6 copy.43
  60.4 3.1 convolution_bitcast_fusion.5
  64.9 80.9 %reduce-scatter.15.cloned.1.call-done = f32[1,1,128,128]{3,2,0,1:T(8,128)} async-done(((f32[1,16,128,128]{3,2,0,1:T(8,128)}), f32[1,1,128,128]{3,2,0,1:T(8,128)}) %reduce-scatter.15.cloned.1.call-update) | async-done | bytes 65552 | tf_op jit(solution)/shard_map/reduce_scatter | solution.py:37
  146.8 18.9 %all_gather.12 = bf16[1,16,128,128]{3,2,0,1:T(8,128)(2,1)S(1)} all-gather(bf16[1,1,128,128]{3,2,0,1:T(8,128)(2,1)S(1)} %get-tuple-element.16), channel_id=1, replica_groups=mesh['row'=16,'col'=64] {'row'}, dimensions={1}, use_global_device_ids=true | all-gather | bytes 557056 | tf_op jit(solution)/shard_map/all_gather | solution.py:19
  165.7 2.0 gather_fusion
  167.6 4.4 convolution_bitcast_fusion.3
  172.0 3.6 copy.39
  175.7 3.1 fusion.54
  180.7 240.1 %reduce-scatter.19.cloned.1.call-done = f32[1,1,32,128]{3,2,1,0:T(8,128)} async-done(((f32[1,64,32,128]{3,2,1,0:T(8,128)}), f32[1,1,32,128]{3,2,1,0:T(8,128)}) %reduce-scatter.19.cloned.1.call-update) | async-done | bytes 16400
  422.5 26.2 %all-gather = bf16[2048,128]{1,0:T(8,128)(2,1)S(1)} all-gather(bf16[128,128]{1,0:T(8,128)(2,1)S(1)} %fusion.13), channel_id=2, replica_groups=mesh['row'=16,'col'=64] {'row'}, dimensions={0}, use_global_device_ids=true | all-gather | bytes 557056 | tf_op jit(solution)/shard_map/all_gather | solution.py:19
  448.7 2.0 gather_fusion.2
  450.6 4.4 convolution_bitcast_fusion.1
  455.0 3.6 copy.47
  458.6 3.1 fusion.52
  463.4 37.1 %all-gather.1 = bf16[2048,128]{1,0:T(8,128)(2,1)S(1)} all-gather(bf16[32,128]{1,0:T(8,128)(2,1)S(1)} %fusion.14), channel_id=3, replica_groups=mesh['row'=16,'col'=64] {'col'}, dimensions={0}, use_global_device_ids=true | all-gather | bytes 532480 | tf_op jit(solution)/shard_map/all_gather | solution.py:16
  500.5 2.0 gather_fusion.3
  502.5 3.8 convolution_bitcast_fusion
  506.3 3.6 copy.50
  509.9 3.1 convolution_bitcast_fusion.4
  514.3 186.5 %reduce-scatter.21.cloned.1.call-done = f32[1,1,32,128]{3,2,1,0:T(8,128)} async-done(((f32[1,64,32,128]{3,2,1,0:T(8,128)}), f32[1,1,32,128]{3,2,1,0:T(8,128)}) %reduce-scatter.21.cloned.1.call-update) | async-done | bytes 16400
  702.2 67.7 %reduce-scatter.17.cloned.1.call-done = f32[1,1,128,128]{3,2,0,1:T(8,128)} async-done(((f32[1,16,128,128]{3,2,0,1:T(8,128)}), f32[1,1,128,128]{3,2,0,1:T(8,128)}) %reduce-scatter.17.cloned.1.call-update) | async-done | bytes 65552 | tf_op jit(solution)/shard_map/reduce_scatter | solution.py:37
  (53 shorter events, 14.8 us)
Async XLA Ops:
  7.2 45.2 %copy-start = (bf16[1,1,48,128,128]{4,3,2,1,0:T(8,128)(2,1)S(1)}, bf16[1,1,48,128,128]{4,3,2,1,0:T(8,128)(2,1)}, u32[]{:S(2)}) copy-start(bf16[1,1,48,128,128]{4,3,2,1,0:T(8,128)(2,1)} %param.17) | copy-start | bytes 4718596
  7.2 138.6 %reduce-scatter.15.cloned.1.call-start = ((), (), s32[]{:S(2)}) async-start(), calls=%async_computation.4 | async-start | bytes 1114112 | tf_op jit(solution)/shard_map/reduce_scatter | solution.py:37
  56.1 4.3 copy-start.8
  63.5 1.4 copy-start.9
  63.5 82.3 %copy-start.2 = (bf16[1,1,128,128]{3,2,1,0:T(8,128)(2,1)S(1)}, bf16[1,1,128,128]{3,2,1,0:T(8,128)(2,1)}, u32[]{:S(2)}) copy-start(bf16[1,1,128,128]{3,2,1,0:T(8,128)(2,1)} %param.14) | copy-start | bytes 98308
  64.8 355.9 %reduce-scatter.19.cloned.1.call-start = ((), (), s32[]{:S(2)}) async-start(), calls=%async_computation.6 | async-start | bytes 1064960
  146.8 33.6 %copy-start.1 = (bf16[1,1,128,128]{3,2,1,0:T(8,128)(2,1)}, bf16[1,1,128,128]{3,2,1,0:T(8,128)(2,1)S(1)}, u32[]{:S(2)}) copy-start(bf16[1,1,128,128]{3,2,1,0:T(8,128)(2,1)S(1)} %get-tuple-element.15) | copy-start | bytes 98308
  172.0 3.6 copy-start.7
  178.7 1.4 copy-start.4
  178.7 1.7 copy-start.5
  178.7 242.8 %copy-start.6 = (s32[1,1,256]{2,1,0:T(1,128)S(1)}, s32[1,1,256]{2,1,0:T(1,128)}, u32[]{:S(2)}) copy-start(s32[1,1,256]{2,1,0:T(1,128)} %param.21) | copy-start | bytes 3076
  180.1 520.7 %reduce-scatter.21.cloned.1.call-start = ((), (), s32[]{:S(2)}) async-start(), calls=%async_computation.7 | async-start | bytes 1064960
  421.5 29.1 %copy-start.3 = (bf16[1,1,32,128]{3,2,1,0:T(8,128)(2,1)}, bf16[1,1,32,128]{3,2,1,0:T(8,128)(2,1)S(1)}, u32[]{:S(2)}) copy-start(bf16[1,1,32,128]{3,2,1,0:T(8,128)(2,1)S(1)} %multiply_convert_fusion.2) | copy-start | bytes 24580
  463.0 306.9 %reduce-scatter.17.cloned.1.call-start = ((), (), s32[]{:S(2)}) async-start(), calls=%async_computation.5 | async-start | bytes 1114112 | tf_op jit(solution)/shard_map/reduce_scatter | solution.py:37
Sparse Core Ops, SparseCore 0:
  64.9 80.8 reduce-scatter.14
  180.2 240.4 reduce-scatter.18
  463.2 237.5 reduce-scatter.20
  704.4 65.4 reduce-scatter.16
where the time goes:
time: 781 us; the launch traced here: 778 us
  waiting for transfers between devices  575 us (74%)
  blocking collectives  123 us (16%)
  matrix products  30.4 us (4%)
  local copies, waits for them, and re-layouts  27.5 us (4%)
  between operations  14.6 us (2%)
    unnamed x6, waiting for transfers between devices  427 us
    reduce_scatter x2, waiting for transfers between devices, propagate(): lax.psum_scatter(item_part.reshape(1, nrow, item_cnt, width), 'row', scat...  149 us
    all_gather x2, blocking collectives, propagate(): lax.all_gather(scaled_users, 'col', axis=1, tiled=True)  77.4 us
    all_gather x2, blocking collectives, propagate(): lax.all_gather(scaled_items, 'row', axis=1, tiled=True)  45.1 us
  transfers between devices with their start and end apart: 4, of which 4 were waited for; matrix products, arithmetic and copies ran while one was open for 2% of the time, Pallas kernels for 0%

commit v1 on v0

v1 whole, which is shorter than its diff:
```python
import jax
import jax.numpy as jnp
from jax import lax
from jax.experimental import pallas as pl
from jax.experimental.pallas import tpu as pltpu
from jax.sharding import PartitionSpec as P

MESH = pl.DeviceIdType.MESH
F32, BF16, I32 = jnp.float32, jnp.bfloat16, jnp.int32
D = 128
TB = 128
UC = 32
HU = UC // 2
IC = 128
TILES = 48
BPR = 256
NX, NY, NZ = 8, 8, 8
TROWS = NX * NY * UC // TB
TCOLS = NZ * 2 * IC // TB
STOP = 99

SEM = pltpu.SemaphoreType.DMA


def each(n, body):
    lax.fori_loop(0, n, lambda i, c: (body(i), c)[1], 0)


def await_bytes(ref, sem):
    pltpu.make_async_copy(ref, ref, sem).wait()


def column(row, n, start=0):
    i = lax.broadcasted_iota(I32, (n, n), 0)
    j = lax.broadcasted_iota(I32, (n, n), 1)
    return jnp.sum(jnp.where(i == j, jnp.broadcast_to(row, (n, n)), 0), axis=1, keepdims=True)


def inv_sqrt(x):
    y = lax.rsqrt(x)
    return y * (1.5 - 0.5 * x * y * y)


def slot_order(key_row, other_row, live, order_ref):
    n = TILES
    key_row = jnp.where(live, key_row, 1024)
    key = column(key_row, n)
    other = column(other_row, n)
    sub = lax.broadcasted_iota(I32, (n, n), 0)
    lane = lax.broadcasted_iota(I32, (n, n), 1)
    rows = jnp.broadcast_to(key_row, (n, n))
    tied = (rows == key) & (lane < sub)
    rank = jnp.sum(jnp.where((rows < key) | tied, 1, 0), axis=1, keepdims=True)
    follows = jnp.max(jnp.where(tied, 1, 0), axis=1, keepdims=True)
    place = lax.broadcasted_iota(I32, (n, 128), 1)
    slot = lax.broadcasted_iota(I32, (n, 128), 0)
    hit = place == rank
    order_ref[0:1, :] = jnp.sum(jnp.where(hit, slot, 0), axis=0, keepdims=True)
    order_ref[1:2, :] = jnp.sum(jnp.where(hit, other, 0), axis=0, keepdims=True)
    order_ref[2:3, :] = jnp.sum(jnp.where(hit, follows, 0), axis=0, keepdims=True)
    upto = jnp.sum(jnp.where(key <= place, 1, 0), axis=0, keepdims=True)
    order_ref[3:4, :] = jnp.maximum(upto - 1, 0)
    order_ref[4:5, :] = jnp.max(jnp.where(key == place, 1, 0), axis=0, keepdims=True)


def kernel(
    users, items, udeg, ideg, tiles, trows, tcols, tcount, bu, bp, bn,
    user_out, item_out, grad_users, grad_items,
    tv, tt, ordr_v, ordc_v, ordr, ordc, part,
    huT, hu, hdT, hd, upad,
    uf0, uf1, itf0, itf1,
    pu0, pu1, pi0, pi1,
    ra0, rb0, ra1, rb1,
    sa0, sb0, sa1, sb1,
    qa0, qb0, qa1, qb1,
    rp0, rp1, si0, si1, si1f, rz0, rz1,
    load_sem, ag_sem, ag_zs, rs_sem, rs_ps,
):
    r = lax.axis_index("row")
    c = lax.axis_index("col")
    core = lax.rem(r, 2)
    z = lax.div(r, 2)
    x = lax.rem(c, NX)
    y = lax.div(c, NX)

    def at_x(k):
        xx = lax.rem(x + k, NX)
        return xx, (r, y * NX + xx)

    def at_y(k):
        yy = lax.rem(y + k, NY)
        return yy, (r, yy * NX + x)

    def at_z(k):
        zz = lax.rem(z + k, NZ)
        return zz, (zz * 2 + core, c)

    partner = (z * 2 + 1 - core, c)

    def send(src, dst, ssem, rsem, device):
        pltpu.make_async_remote_copy(
            src_ref=src, dst_ref=dst, send_sem=ssem, recv_sem=rsem, device_id=device, device_id_type=MESH
        ).start()

    tile_load = pltpu.make_async_copy(tiles, tv, load_sem)
    tile_load.start()

    barrier = pltpu.get_barrier_semaphore()

    def greet(device):
        pl.semaphore_signal(barrier, inc=1, device_id=device, device_id_type=MESH)

    greet(partner)
    each(NX - 1, lambda k: greet(at_x(k + 1)[1]))
    each(NY - 1, lambda k: greet(at_y(k + 1)[1]))
    each(NZ - 1, lambda k: greet(at_z(k + 1)[1]))

    du = inv_sqrt(column(udeg[...], UC).astype(F32))
    di = inv_sqrt(column(ideg[...], IC).astype(F32))

    def gather_start(q, uf, itf, user_val, item_val):
        uf[y, x] = (user_val * du).astype(BF16)
        itf[z, core] = (item_val * di).astype(BF16)
        if q == 0:
            pl.semaphore_wait(barrier, NX + NY + NZ - 2)
        s = ag_sem.at[q]

        def one_z(k):
            zz, dev = at_z(k + 1)
            own = itf.at[z, core]
            send(own, own, s.at[0], ag_zs.at[q, k], dev)

        def one_x(k):
            own = uf.at[y, x, 0:HU]
            send(own, own, s.at[3], s.at[4], at_x(k + 1)[1])

        def one_y(k):
            own = uf.at[y, x, HU:UC]
            send(own, own, s.at[5], s.at[6], at_y(k + 1)[1])

        each(NX - 1, one_x)
        each(NY - 1, one_y)
        each(NZ - 1, one_z)
        own = itf.at[z, core]
        send(own, own, s.at[1], s.at[2], partner)

    def gather_second(q, uf):
        s = ag_sem.at[q]
        await_bytes(uf.at[0, 0 : NX - 1, 0:HU], s.at[4])

        def one_y(k):
            own = uf.at[y, :, 0:HU]
            send(own, own, s.at[7], s.at[8], at_y(k + 1)[1])

        each(NY - 1, one_y)
        await_bytes(uf.at[0 : NY - 1, 0, HU:UC], s.at[6])

        def one_x(k):
            own = uf.at[:, x, HU:UC]
            send(own, own, s.at[9], s.at[10], at_x(k + 1)[1])

        each(NX - 1, one_x)

    def gather_forward(q, itf):
        s = ag_sem.at[q]

        def one(k):
            zz = lax.rem(z + NZ - 1 - k, NZ)
            got = itf.at[zz, core]
            await_bytes(got, ag_zs.at[q, k])
            send(got, got, s.at[1], s.at[2], partner)

        each(NZ - 1, one)

    def gather_items_done(q, itf):
        await_bytes(itf.at[:, 0], ag_sem.at[q, 2])

    def gather_users_done(q, uf):
        await_bytes(uf.at[0 : NY - 1, :, 0:HU], ag_sem.at[q, 8])
        await_bytes(uf.at[:, 0 : NX - 1, HU:UC], ag_sem.at[q, 10])

    def gather_sent(q, uf, itf):
        s = ag_sem.at[q]
        await_bytes(itf.at[0 : NZ - 1, 0], s.at[0])
        await_bytes(itf.at[:, 0], s.at[1])
        await_bytes(uf.at[0, 0 : NX - 1, 0:HU], s.at[3])
        await_bytes(uf.at[0 : NY - 1, 0, HU:UC], s.at[5])
        await_bytes(uf.at[0 : NY - 1, :, 0:HU], s.at[7])
        await_bytes(uf.at[:, 0 : NX - 1, HU:UC], s.at[9])

    def user_side(itf, pu):
        def one(j, acc):
            other = ordr[1, j]
            block = itf[lax.div(other, 2), lax.rem(other, 2)]
            prod = jnp.dot(tv[ordr[0, j]], block, preferred_element_type=F32)
            acc = acc * ordr[2, j].astype(F32) + prod
            part[j] = acc
            return acc

        lax.fori_loop(0, TILES, one, jnp.zeros((TB, D), F32), unroll=4)

        def place(t):
            whole = part[ordr[3, t]] * ordr[4, t].astype(F32)
            per = NX * UC // TB
            cols = TB // UC
            yy = lax.div(t, per)
            xx = lax.rem(t, per) * cols
            pu[yy, pl.ds(xx, cols)] = whole.reshape(cols, UC, D).astype(pu.dtype)

        each(TROWS, place)

    def item_side(uf, pi):
        def one(j, acc):
            t = ordc[1, j]
            per = NX * UC // TB
            cols = TB // UC
            block = uf[lax.div(t, per), pl.ds(lax.rem(t, per) * cols, cols)].reshape(TB, D)
            prod = jnp.dot(tt[j], block, preferred_element_type=F32)
            acc = acc * ordc[2, j].astype(F32) + prod
            part[j] = acc
            return acc

        lax.fori_loop(0, TILES, one, jnp.zeros((TB, D), F32), unroll=4)

        def place(t):
            pi[lax.div(t, 2), lax.rem(t, 2)] = part[ordc[3, t]] * ordc[4, t].astype(F32)

        each(TCOLS, place)

    def scatter_users_first(q, pu, ra, rb):
        s = rs_sem.at[q]

        def one_y(k):
            yy, dev = at_y(k + 1)
            send(pu.at[yy, :, 0:HU], ra.at[k], s.at[0], s.at[1], dev)

        def one_x(k):
            xx, dev = at_x(k + 1)
            send(pu.at[:, xx, HU:UC], rb.at[k], s.at[2], s.at[3], dev)

        each(NY - 1, one_y)
        each(NX - 1, one_x)

    def scatter_users_second(q, pu, ra, rb, sa, sb, qa, qb):
        s = rs_sem.at[q]
        await_bytes(ra, s.at[1])
        sa[...] = pu[y, :, 0:HU].astype(F32) + jnp.sum(ra[...].astype(F32), axis=0)

        def one_x(k):
            xx, dev = at_x(k + 1)
            send(sa.at[xx], qa.at[k], s.at[4], s.at[5], dev)

        each(NX - 1, one_x)
        await_bytes(rb, s.at[3])
        sb[...] = pu[:, x, HU:UC].astype(F32) + jnp.sum(rb[...].astype(F32), axis=0)

        def one_y(k):
            yy, dev = at_y(k + 1)
            send(sb.at[yy], qb.at[k], s.at[6], s.at[7], dev)

        each(NY - 1, one_y)

    def scatter_users_done(q, sa, sb, qa, qb):
        s = rs_sem.at[q]
        await_bytes(qa, s.at[5])
        await_bytes(qb, s.at[7])
        first = sa[x] + jnp.sum(qa[...], axis=0)
        second = sb[y] + jnp.sum(qb[...], axis=0)
        return jnp.concatenate([first, second], axis=0) * du

    def scatter_users_sent(q, ra, rb, qa, qb):
        s = rs_sem.at[q]
        await_bytes(ra, s.at[0])
        await_bytes(rb, s.at[2])
        await_bytes(qa, s.at[4])
        await_bytes(qb, s.at[6])

    def scatter_items_first(q, pi, rp):
        s = rs_sem.at[q]

        def one(k):
            zz = lax.rem(z + 1 + k, NZ)
            send(pi.at[zz, 1 - core], rp.at[zz], s.at[8], rs_ps.at[q, k], partner)

        each(NZ, one)

    def scatter_items_second(q, pi, rp, si, keep, rz):
        s = rs_sem.at[q]

        def one(k):
            zz, dev = at_z(k + 1)
            await_bytes(rp.at[zz], rs_ps.at[q, k])
            si[zz] = (pi[zz, core] + rp[zz]).astype(si.dtype)
            send(si.at[zz], rz.at[k], s.at[9], s.at[10], dev)

        each(NZ - 1, one)
        await_bytes(rp.at[z], rs_ps.at[q, NZ - 1])
        keep[...] = pi[z, core] + rp[z]

    def scatter_items_done(q, keep, rz):
        await_bytes(rz, rs_sem.at[q, 10])
        return (keep[...] + jnp.sum(rz[...].astype(F32), axis=0)) * di

    def scatter_items_sent(q, rp, rz):
        await_bytes(rp, rs_sem.at[q, 8])
        await_bytes(rz, rs_sem.at[q, 9])

    gather_start(0, uf0, itf0, users[...].astype(F32), items[...].astype(F32))
    live = lax.broadcasted_iota(I32, (1, TILES), 1) < tcount[0, 0]
    slot_order(trows[...], tcols[...], live, ordr_v)
    slot_order(tcols[...], trows[...], live, ordc_v)
    copy_r = pltpu.make_async_copy(ordr_v, ordr, load_sem)
    tile_load.wait()
    copy_r.start()
    copy_r.wait()
    copy_c = pltpu.make_async_copy(ordc_v, ordc, load_sem)
    copy_c.start()
    copy_c.wait()
    gather_second(0, uf0)
    gather_forward(0, itf0)

    def turn(j):
        tt[j] = tv[ordc[0, j]].T

    each(TILES, turn)

    ids = lax.broadcasted_iota(I32, (IC, BPR), 0)
    hot_u = jnp.where(ids == bu[...], 1.0, 0.0)
    hot_d = jnp.where(ids == bp[...], 1.0, 0.0) - jnp.where(ids == bn[...], 1.0, 0.0)
    huT[...] = hot_u[0:UC].astype(BF16)
    hdT[...] = hot_d.astype(BF16)
    hu[...] = hot_u.T.astype(BF16)
    hd[...] = hot_d.T.astype(BF16)

    gather_items_done(0, itf0)
    user_side(itf0, pu0)
    scatter_users_first(0, pu0, ra0, rb0)
    gather_users_done(0, uf0)
    item_side(uf0, pi0)
    scatter_items_first(0, pi0, rp0)
    scatter_users_second(0, pu0, ra0, rb0, sa0, sb0, qa0, qb0)
    scatter_items_second(0, pi0, rp0, si0, si0.at[z], rz0)
    u_out = scatter_users_done(0, sa0, sb0, qa0, qb0).astype(BF16)
    i_out = scatter_items_done(0, si0.at[z], rz0).astype(BF16)
    user_out[...] = u_out
    item_out[...] = i_out

    upad[0:UC] = u_out
    upad[UC:IC] = jnp.zeros((IC - UC, D), BF16)
    u_vec = jnp.dot(hu[...], upad[...], preferred_element_type=F32)
    d_vec = jnp.dot(hd[...], i_out, preferred_element_type=F32)
    score = jnp.sum(u_vec * d_vec, axis=1, keepdims=True)
    weight = -jax.nn.sigmoid(-score)

    def spread(hotT, v):
        hi = v.astype(BF16)
        lo = (v - hi.astype(F32)).astype(BF16)
        return jnp.dot(hotT, hi, preferred_element_type=F32) + jnp.dot(hotT, lo, preferred_element_type=F32)

    g_u = spread(huT[...], weight * d_vec)
    g_i = spread(hdT[...], weight * u_vec)

    gather_start(1, uf1, itf1, g_u, g_i)
    gather_second(1, uf1)
    gather_forward(1, itf1)
    gather_items_done(1, itf1)
    user_side(itf1, pu1)
    scatter_users_first(1, pu1, ra1, rb1)
    gather_users_done(1, uf1)
    item_side(uf1, pi1)
    scatter_items_first(1, pi1, rp1)
    scatter_users_second(1, pu1, ra1, rb1, sa1, sb1, qa1, qb1)
    scatter_items_second(1, pi1, rp1, si1, si1f, rz1)
    grad_users[...] = scatter_users_done(1, sa1, sb1, qa1, qb1)
    grad_items[...] = scatter_items_done(1, si1f, rz1)

    gather_sent(0, uf0, itf0)
    gather_sent(1, uf1, itf1)
    scatter_users_sent(0, ra0, rb0, qa0, qb0)
    scatter_users_sent(1, ra1, rb1, qa1, qb1)
    scatter_items_sent(0, rp0, rz0)
    scatter_items_sent(1, rp1, rz1)


def local(users, items, udeg, ideg, tiles, trows, tcols, tcount, bu, bp, bn):
    vmem = pl.BlockSpec(memory_space=pltpu.VMEM)
    smem = pl.BlockSpec(memory_space=pltpu.SMEM)
    hbm = pl.BlockSpec(memory_space=pl.ANY)
    V = pltpu.VMEM
    order = (8, 128)
    fields = (NY, NX, UC, D)
    fieldi = (NZ, 2, IC, D)
    outs = pl.pallas_call(
        kernel,
        out_shape=(
            jax.ShapeDtypeStruct((UC, D), BF16),
            jax.ShapeDtypeStruct((IC, D), BF16),
            jax.ShapeDtypeStruct((UC, D), F32),
            jax.ShapeDtypeStruct((IC, D), F32),
        ),
        in_specs=[vmem, vmem, vmem, vmem, hbm, vmem, vmem, smem, vmem, vmem, vmem],
        out_specs=(vmem,) * 4,
        scratch_shapes=[
            V((TILES, TB, TB), BF16),
            V((TILES, TB, TB), BF16),
            V(order, I32),
            V(order, I32),
            pltpu.SMEM(order, I32),
            pltpu.SMEM(order, I32),
            V((TILES, TB, D), F32),
            V((UC, BPR), BF16),
            V((BPR, IC), BF16),
            V((IC, BPR), BF16),
            V((BPR, IC), BF16),
            V((IC, D), BF16),
            V(fields, BF16),
            V(fields, BF16),
            V(fieldi, BF16),
            V(fieldi, BF16),
            V(fields, F32),
            V(fields, BF16),
            V(fieldi, F32),
            V(fieldi, F32),
            V((NY - 1, NX, HU, D), F32),
            V((NX - 1, NY, HU, D), F32),
            V((NY - 1, NX, HU, D), BF16),
            V((NX - 1, NY, HU, D), BF16),
            V((NX, HU, D), F32),
            V((NY, HU, D), F32),
            V((NX, HU, D), F32),
            V((NY, HU, D), F32),
            V((NX - 1, HU, D), F32),
            V((NY - 1, HU, D), F32),
            V((NX - 1, HU, D), F32),
            V((NY - 1, HU, D), F32),
            V((NZ, IC, D), F32),
            V((NZ, IC, D), F32),
            V((NZ, IC, D), F32),
            V((NZ, IC, D), BF16),
            V((IC, D), F32),
            V((NZ - 1, IC, D), F32),
            V((NZ - 1, IC, D), BF16),
            SEM,
            SEM((2, 11)),
            SEM((2, NZ - 1)),
            SEM((2, 11)),
            SEM((2, NZ)),
        ],
        compiler_params=pltpu.CompilerParams(
            collective_id=0, has_side_effects=True, vmem_limit_bytes=48 * 1024 * 1024
        ),
        name="lightgcn",
    )(
        users[0, 0], items[0, 0], udeg[0], ideg[0], tiles[0, 0], trows[0], tcols[0], tcount, bu[0], bp[0], bn[0]
    )
    return tuple(o[None, None] for o in outs)


def solution(mesh):
    u2, i2 = P("row", "col"), P("col", "row")
    return jax.shard_map(
        local,
        mesh=mesh,
        in_specs=(u2, i2, u2, i2, u2, u2, u2, u2, u2, u2, u2),
        out_specs=(u2, i2, u2, i2),
        check_vma=False,
    )
```

time: 781 us -> 106 us (0.14)
  waiting for transfers between devices: 575 us -> 0 us
  blocking collectives: 123 us -> 0 us
  Pallas kernels: 0 us -> 94.4 us
  matrix products: 30.4 us -> 0 us
  local copies, waits for them, and re-layouts: 27.5 us -> 9.96 us
  between operations: 14.6 us -> 1.31 us
    unnamed x6 -> x0, waiting for transfers between devices: 427 us -> none
    reduce_scatter x2 -> x0, waiting for transfers between devices: 149 us -> none  [propagate(): lax.psum_scatter(item_part.reshape(1, nrow, item_cnt, width), 'row', scat...]
    all_gather x4 -> x0, blocking collectives: 123 us -> none  [the longest x2 77.4 us: propagate(): lax.all_gather(scaled_users, 'col', axis=1, tiled=True)]
    pallas_call x0 -> x1, Pallas kernels: none -> 94.4 us  [local(): pl.pallas_call(kernel, out_shape=(jax.ShapeDtypeStruct((UC, D), BF16), ja...]
    dot_general x14 -> x0, matrix products: 30.4 us -> none  [the longest x2 8.81 us: propagate(): jnp.einsum('sab,sbd->sad', tiles, item_blocks, preferred_element_type=jnp...]
    dot_general x6 -> x0, local copies, waits for them, and re-layouts: 17 us -> none  [the longest x2 7.22 us: propagate(): jnp.einsum('sab,sad->sbd', tiles, user_blocks, preferred_element_type=jnp...]
    unnamed x20 -> x24, local copies, waits for them, and re-layouts: 0.06 us -> 9.96 us
    gather x4 -> x0, local copies, waits for them, and re-layouts: 7.81 us -> none  [the longest x2 3.91 us: propagate(): user_blocks = jnp.take(user_region, rows, axis=0)]
  transfers between devices with their start and end apart: 4 -> 0, of which waited for: 4 -> 0; matrix products, arithmetic and copies ran while one was open for 2% -> 0% of each run, Pallas kernels for 0% -> 0%
where the time goes in v1:
time: 106 us
  Pallas kernels  94.4 us (89%)
  local copies, waits for them, and re-layouts  9.96 us (9%)
  between operations  1.31 us (1%)
    pallas_call x1, Pallas kernels, local(): pl.pallas_call(kernel, out_shape=(jax.ShapeDtypeStruct((UC, D), BF16), ja...  94.4 us
    unnamed x24, local copies, waits for them, and re-layouts  9.96 us

profile of v1, /device:TPU:1, one launch (start us, length us, event | category | flops | bytes accessed | tf_op | source)
XLA Modules:
  0.0 105.6 jit_solution(8273224820515583631)
XLA Ops:
  1.3 0.0 copy-start
  1.3 1.4 %copy-done = bf16[1,1,48,128,128]{4,3,2,1,0:T(8,128)(2,1)S(1)} copy-done((bf16[1,1,48,128,128]{4,3,2,1,0:T(8,128)(2,1)S(1)}, bf16[1,1,48,128,128]{4,3,2,1,0:T(8,128)(2,1)}, u32[]{:S(2)}) %copy-start) | copy-done | bytes 1572888
  2.7 0.0 copy-start.1
  2.7 0.8 copy-done.1
  3.4 0.0 copy-start.2
  3.5 0.7 copy-done.2
  4.1 0.0 copy-start.3
  4.1 0.7 copy-done.3
  4.8 0.0 copy-start.4
  4.8 0.7 copy-done.4
  5.5 0.0 copy-start.5
  5.5 0.7 copy-done.5
  6.2 0.0 copy-start.6
  6.2 0.7 copy-done.6
  6.8 0.0 copy-start.7
  6.8 0.7 copy-done.7
  7.5 0.7 copy-done.8
  8.2 0.0 copy-start.9
  8.2 0.7 copy-done.9
  8.8 94.4 %lightgcn.1 = (bf16[32,128]{1,0:T(8,128)(2,1)S(1)}, bf16[128,128]{1,0:T(8,128)(2,1)S(1)}, f32[32,128]{1,0:T(8,128)S(1)}, f32[128,128]{1,0:T(8,128)S(1)}) custom-call(bf16[32,128]{1,0:T(8,128)(2,1)S(1)} %bitcast.19, bf16[128,128]{1,0:T(8,128)(2,1)S(1)} %bitcast.17, s32[1,32]{1,0:T(1,128)S(1)} %bitcast.24, s32[1,128]{1,0:T(1,128)S(1)} %bitcast.25, ...), custom_call_target="tpu_custom_call" | custom-call | tf_op jit(solution)/shard_map/lightgcn/pallas_call | solution.py:393
  103.2 0.6 copy.20
  103.8 0.6 copy.21
  104.4 0.6 copy.22
  105.0 0.6 copy.23
  (1 shorter events, 0.0 us)
Async XLA Ops:
  1.3 1.4 %copy-start = (bf16[1,1,48,128,128]{4,3,2,1,0:T(8,128)(2,1)S(1)}, bf16[1,1,48,128,128]{4,3,2,1,0:T(8,128)(2,1)}, u32[]{:S(2)}) copy-start(bf16[1,1,48,128,128]{4,3,2,1,0:T(8,128)(2,1)} %param.15) | copy-start | bytes 4718596
  2.7 0.8 copy-start.1
  3.4 0.7 copy-start.2
  4.1 0.7 copy-start.3
  4.8 0.7 copy-start.4
  5.5 0.7 copy-start.5
  6.2 0.7 copy-start.6
  6.8 0.7 copy-start.7
  7.5 0.7 copy-start.8
  8.2 0.7 copy-start.9

commit v2 on v1

--- a/solution.py
+++ b/solution.py
@@ -17,13 +17,24 @@
 NX, NY, NZ = 8, 8, 8
 TROWS = NX * NY * UC // TB
 TCOLS = NZ * 2 * IC // TB
-STOP = 99
+
+NEAR_FIRST = (0, 6, 1, 5, 2, 4, 3)
+FAR_FIRST = (2, 1, 3, 0)
+UNROLL = 16
 
 SEM = pltpu.SemaphoreType.DMA
 
 
 def each(n, body):
     lax.fori_loop(0, n, lambda i, c: (body(i), c)[1], 0)
+
+
+def each_far_first(n, body):
+    def one(i):
+        off = lax.div(i + 1, 2)
+        body(n // 2 + off * (1 - 2 * lax.rem(i, 2)))
+
+    each(n, one)
 
 
 def await_bytes(ref, sem):
@@ -64,9 +75,10 @@
 
 
 def kernel(
-    users, items, udeg, ideg, tiles, trows, tcols, tcount, bu, bp, bn,
+    users_h, items_h, udeg_h, ideg_h, tiles_h, trows_h, tcols_h, tcount_h, bu_h, bp_h, bn_h,
     user_out, item_out, grad_users, grad_items,
-    tv, tt, ordr_v, ordc_v, ordr, ordc, part,
+    users, items, udeg, ideg, tv, trows, tcols, tcount, bu, bp, bn,
+    tt, ordr_v, ordc_v, ordr, ordc, part,
     huT, hu, hdT, hd, upad,
     uf0, uf1, itf0, itf1,
     pu0, pu1, pi0, pi1,
@@ -74,7 +86,7 @@
     sa0, sb0, sa1, sb1,
     qa0, qb0, qa1, qb1,
     rp0, rp1, si0, si1, si1f, rz0, rz1,
-    load_sem, ag_sem, ag_zs, rs_sem, rs_ps,
+    load_sem, ag_sem, ag_xs, ag_ys, ag_zs, rs_sem, rs_as, rs_bs, rs_ps,
 ):
     r = lax.axis_index("row")
     c = lax.axis_index("col")
@@ -102,8 +114,13 @@
             src_ref=src, dst_ref=dst, send_sem=ssem, recv_sem=rsem, device_id=device, device_id_type=MESH
         ).start()
 
-    tile_load = pltpu.make_async_copy(tiles, tv, load_sem)
-    tile_load.start()
+    pairs = (
+        (users_h, users), (items_h, items), (udeg_h, udeg), (ideg_h, ideg), (tiles_h, tv), (trows_h, trows),
+        (tcols_h, tcols), (tcount_h, tcount), (bu_h, bu), (bp_h, bp), (bn_h, bn),
+    )
+    loads = [pltpu.make_async_copy(src, dst, load_sem.at[n]) for n, (src, dst) in enumerate(pairs)]
+    for n in (2, 3, 0, 1, 5, 6, 7, 4, 8, 9, 10):
+        loads[n].start()
 
     barrier = pltpu.get_barrier_semaphore()
 
@@ -115,6 +132,8 @@
     each(NY - 1, lambda k: greet(at_y(k + 1)[1]))
     each(NZ - 1, lambda k: greet(at_z(k + 1)[1]))
 
+    for n in range(4):
+        loads[n].wait()
     du = inv_sqrt(column(udeg[...], UC).astype(F32))
     di = inv_sqrt(column(ideg[...], IC).astype(F32))
 
@@ -124,69 +143,52 @@
         if q == 0:
             pl.semaphore_wait(barrier, NX + NY + NZ - 2)
         s = ag_sem.at[q]
-
-        def one_z(k):
-            zz, dev = at_z(k + 1)
-            own = itf.at[z, core]
-            send(own, own, s.at[0], ag_zs.at[q, k], dev)
-
-        def one_x(k):
-            own = uf.at[y, x, 0:HU]
-            send(own, own, s.at[3], s.at[4], at_x(k + 1)[1])
-
-        def one_y(k):
-            own = uf.at[y, x, HU:UC]
-            send(own, own, s.at[5], s.at[6], at_y(k + 1)[1])
-
-        each(NX - 1, one_x)
-        each(NY - 1, one_y)
-        each(NZ - 1, one_z)
-        own = itf.at[z, core]
-        send(own, own, s.at[1], s.at[2], partner)
+        mine_u = uf.at[y, x]
+        mine_i = itf.at[z, core]
+
+        def one(k):
+            send(mine_u, mine_u, s.at[3], ag_xs.at[q, k], at_x(k + 1)[1])
+            send(mine_u, mine_u, s.at[5], ag_ys.at[q, k], at_y(k + 1)[1])
+
+        each_far_first(NX - 1, one)
+        each_far_first(NZ - 1, lambda k: send(mine_i, mine_i, s.at[0], ag_zs.at[q, k], at_z(k + 1)[1]))
+        send(mine_i, mine_i, s.at[1], s.at[2], partner)
 
     def gather_second(q, uf):
         s = ag_sem.at[q]
-        await_bytes(uf.at[0, 0 : NX - 1, 0:HU], s.at[4])
-
-        def one_y(k):
-            own = uf.at[y, :, 0:HU]
-            send(own, own, s.at[7], s.at[8], at_y(k + 1)[1])
-
-        each(NY - 1, one_y)
-        await_bytes(uf.at[0 : NY - 1, 0, HU:UC], s.at[6])
-
-        def one_x(k):
-            own = uf.at[:, x, HU:UC]
-            send(own, own, s.at[9], s.at[10], at_x(k + 1)[1])
-
-        each(NX - 1, one_x)
+        for k in NEAR_FIRST:
+            xx = lax.rem(x + NX - 1 - k, NX)
+            await_bytes(uf.at[y, xx], ag_xs.at[q, k])
+            half = uf.at[y, xx, 0:HU]
+            each_far_first(NY - 1, lambda j: send(half, half, s.at[7], s.at[8], at_y(j + 1)[1]))
+            yy = lax.rem(y + NY - 1 - k, NY)
+            await_bytes(uf.at[yy, x], ag_ys.at[q, k])
+            other = uf.at[yy, x, HU:UC]
+            each_far_first(NX - 1, lambda j: send(other, other, s.at[9], s.at[10], at_x(j + 1)[1]))
 
     def gather_forward(q, itf):
         s = ag_sem.at[q]
-
-        def one(k):
+        for k in NEAR_FIRST:
             zz = lax.rem(z + NZ - 1 - k, NZ)
             got = itf.at[zz, core]
             await_bytes(got, ag_zs.at[q, k])
             send(got, got, s.at[1], s.at[2], partner)
 
-        each(NZ - 1, one)
-
     def gather_items_done(q, itf):
         await_bytes(itf.at[:, 0], ag_sem.at[q, 2])
 
     def gather_users_done(q, uf):
-        await_bytes(uf.at[0 : NY - 1, :, 0:HU], ag_sem.at[q, 8])
-        await_bytes(uf.at[:, 0 : NX - 1, HU:UC], ag_sem.at[q, 10])
+        await_bytes(uf.at[0 : NY - 1, 0 : NX - 1, 0:HU], ag_sem.at[q, 8])
+        await_bytes(uf.at[0 : NY - 1, 0 : NX - 1, HU:UC], ag_sem.at[q, 10])
 
     def gather_sent(q, uf, itf):
         s = ag_sem.at[q]
         await_bytes(itf.at[0 : NZ - 1, 0], s.at[0])
         await_bytes(itf.at[:, 0], s.at[1])
-        await_bytes(uf.at[0, 0 : NX - 1, 0:HU], s.at[3])
-        await_bytes(uf.at[0 : NY - 1, 0, HU:UC], s.at[5])
-        await_bytes(uf.at[0 : NY - 1, :, 0:HU], s.at[7])
-        await_bytes(uf.at[:, 0 : NX - 1, HU:UC], s.at[9])
+        await_bytes(uf.at[0, 0 : NX - 1], s.at[3])
+        await_bytes(uf.at[0 : NY - 1, 0], s.at[5])
+        await_bytes(uf.at[0 : NY - 1, 0 : NX - 1, 0:HU], s.at[7])
+        await_bytes(uf.at[0 : NY - 1, 0 : NX - 1, HU:UC], s.at[9])
 
     def user_side(itf, pu):
         def one(j, acc):
@@ -197,7 +199,7 @@
             part[j] = acc
             return acc
 
-        lax.fori_loop(0, TILES, one, jnp.zeros((TB, D), F32), unroll=4)
+        lax.fori_loop(0, TILES, one, jnp.zeros((TB, D), F32), unroll=UNROLL)
 
         def place(t):
             whole = part[ordr[3, t]] * ordr[4, t].astype(F32)
@@ -220,7 +222,7 @@
             part[j] = acc
             return acc
 
-        lax.fori_loop(0, TILES, one, jnp.zeros((TB, D), F32), unroll=4)
+        lax.fori_loop(0, TILES, one, jnp.zeros((TB, D), F32), unroll=UNROLL)
 
         def place(t):
             pi[lax.div(t, 2), lax.rem(t, 2)] = part[ordc[3, t]] * ordc[4, t].astype(F32)
@@ -229,36 +231,48 @@
 
     def scatter_users_first(q, pu, ra, rb):
         s = rs_sem.at[q]
-
-        def one_y(k):
-            yy, dev = at_y(k + 1)
-            send(pu.at[yy, :, 0:HU], ra.at[k], s.at[0], s.at[1], dev)
-
-        def one_x(k):
-            xx, dev = at_x(k + 1)
-            send(pu.at[:, xx, HU:UC], rb.at[k], s.at[2], s.at[3], dev)
-
-        each(NY - 1, one_y)
-        each(NX - 1, one_x)
+        for step in FAR_FIRST:
+            px = lax.rem(lax.div(x, 2) + step, NX // 2)
+            py = lax.rem(lax.div(y, 2) + step, NY // 2)
+
+            def one(k):
+                yy, dev = at_y(k + 1)
+                send(pu.at[yy, pl.ds(px * 2, 2), 0:HU], ra.at[px, k], s.at[0], rs_as.at[q, px], dev)
+                xx, dev = at_x(k + 1)
+                send(pu.at[pl.ds(py * 2, 2), xx, HU:UC], rb.at[py, k], s.at[2], rs_bs.at[q, py], dev)
+
+            each_far_first(NY - 1, one)
 
     def scatter_users_second(q, pu, ra, rb, sa, sb, qa, qb):
         s = rs_sem.at[q]
-        await_bytes(ra, s.at[1])
-        sa[...] = pu[y, :, 0:HU].astype(F32) + jnp.sum(ra[...].astype(F32), axis=0)
-
-        def one_x(k):
-            xx, dev = at_x(k + 1)
-            send(sa.at[xx], qa.at[k], s.at[4], s.at[5], dev)
-
-        each(NX - 1, one_x)
-        await_bytes(rb, s.at[3])
-        sb[...] = pu[:, x, HU:UC].astype(F32) + jnp.sum(rb[...].astype(F32), axis=0)
-
-        def one_y(k):
-            yy, dev = at_y(k + 1)
-            send(sb.at[yy], qb.at[k], s.at[6], s.at[7], dev)
-
-        each(NY - 1, one_y)
+        for step in FAR_FIRST:
+            px = lax.rem(lax.div(x, 2) + step, NX // 2)
+            py = lax.rem(lax.div(y, 2) + step, NY // 2)
+
+            def to_x(xx):
+                k = lax.rem(xx - x + NX, NX) - 1
+                send(sa.at[xx], qa.at[k], s.at[4], s.at[5], (r, y * NX + xx))
+
+            def to_y(yy):
+                k = lax.rem(yy - y + NY, NY) - 1
+                send(sb.at[yy], qb.at[k], s.at[6], s.at[7], (r, yy * NX + x))
+
+            await_bytes(ra.at[px], rs_as.at[q, px])
+            two = pl.ds(px * 2, 2)
+            sa[two] = pu[y, two, 0:HU].astype(F32) + jnp.sum(ra[px].astype(F32), axis=0)
+            if step:
+                to_x(px * 2)
+                to_x(px * 2 + 1)
+            else:
+                to_x(px * 4 + 1 - x)
+            await_bytes(rb.at[py], rs_bs.at[q, py])
+            two = pl.ds(py * 2, 2)
+            sb[two] = pu[two, x, HU:UC].astype(F32) + jnp.sum(rb[py].astype(F32), axis=0)
+            if step:
+                to_y(py * 2)
+                to_y(py * 2 + 1)
+            else:
+                to_y(py * 4 + 1 - y)
 
     def scatter_users_done(q, sa, sb, qa, qb):
         s = rs_sem.at[q]
@@ -282,7 +296,8 @@
             zz = lax.rem(z + 1 + k, NZ)
             send(pi.at[zz, 1 - core], rp.at[zz], s.at[8], rs_ps.at[q, k], partner)
 
-        each(NZ, one)
+        each_far_first(NZ - 1, one)
+        one(NZ - 1)
 
     def scatter_items_second(q, pi, rp, si, keep, rz):
         s = rs_sem.at[q]
@@ -293,7 +308,7 @@
             si[zz] = (pi[zz, core] + rp[zz]).astype(si.dtype)
             send(si.at[zz], rz.at[k], s.at[9], s.at[10], dev)
 
-        each(NZ - 1, one)
+        each_far_first(NZ - 1, one)
         await_bytes(rp.at[z], rs_ps.at[q, NZ - 1])
         keep[...] = pi[z, core] + rp[z]
 
@@ -305,25 +320,36 @@
         await_bytes(rp, rs_sem.at[q, 8])
         await_bytes(rz, rs_sem.at[q, 9])
 
+    def products(q, uf, itf, pu, pi, ra, rb, rp, si, keep, rz):
+        gather_items_done(q, itf)
+        user_side(itf, pu)
+        scatter_users_first(q, pu, ra, rb)
+        gather_users_done(q, uf)
+        item_side(uf, pi)
+        scatter_items_first(q, pi, rp)
+        scatter_items_second(q, pi, rp, si, keep, rz)
+
     gather_start(0, uf0, itf0, users[...].astype(F32), items[...].astype(F32))
-    live = lax.broadcasted_iota(I32, (1, TILES), 1) < tcount[0, 0]
+    for n in range(5, 8):
+        loads[n].wait()
+    live = lax.broadcasted_iota(I32, (1, TILES), 1) < jnp.broadcast_to(tcount[...], (1, TILES))
     slot_order(trows[...], tcols[...], live, ordr_v)
     slot_order(tcols[...], trows[...], live, ordc_v)
-    copy_r = pltpu.make_async_copy(ordr_v, ordr, load_sem)
-    tile_load.wait()
+    copy_r = pltpu.make_async_copy(ordr_v, ordr, load_sem.at[11])
+    copy_c = pltpu.make_async_copy(ordc_v, ordc, load_sem.at[12])
     copy_r.start()
+    copy_c.start()
+    gather_second(0, uf0)
     copy_r.wait()
-    copy_c = pltpu.make_async_copy(ordc_v, ordc, load_sem)
-    copy_c.start()
     copy_c.wait()
-    gather_second(0, uf0)
-    gather_forward(0, itf0)
+    loads[4].wait()
 
     def turn(j):
         tt[j] = tv[ordc[0, j]].T
 
     each(TILES, turn)
-
+    for n in range(8, 11):
+        loads[n].wait()
     ids = lax.broadcasted_iota(I32, (IC, BPR), 0)
     hot_u = jnp.where(ids == bu[...], 1.0, 0.0)
     hot_d = jnp.where(ids == bp[...], 1.0, 0.0) - jnp.where(ids == bn[...], 1.0, 0.0)
@@ -331,15 +357,9 @@
     hdT[...] = hot_d.astype(BF16)
     hu[...] = hot_u.T.astype(BF16)
     hd[...] = hot_d.T.astype(BF16)
-
-    gather_items_done(0, itf0)
-    user_side(itf0, pu0)
-    scatter_users_first(0, pu0, ra0, rb0)
-    gather_users_done(0, uf0)
-    item_side(uf0, pi0)
-    scatter_items_first(0, pi0, rp0)
+    gather_forward(0, itf0)
+    products(0, uf0, itf0, pu0, pi0, ra0, rb0, rp0, si0, si0.at[z], rz0)
     scatter_users_second(0, pu0, ra0, rb0, sa0, sb0, qa0, qb0)
-    scatter_items_second(0, pi0, rp0, si0, si0.at[z], rz0)
     u_out = scatter_users_done(0, sa0, sb0, qa0, qb0).astype(BF16)
     i_out = scatter_items_done(0, si0.at[z], rz0).astype(BF16)
     user_out[...] = u_out
@@ -363,14 +383,8 @@
     gather_start(1, uf1, itf1, g_u, g_i)
     gather_second(1, uf1)
     gather_forward(1, itf1)
-    gather_items_done(1, itf1)
-    user_side(itf1, pu1)
-    scatter_users_first(1, pu1, ra1, rb1)
-    gather_users_done(1, uf1)
-    item_side(uf1, pi1)
-    scatter_items_first(1, pi1, rp1)
+    products(1, uf1, itf1, pu1, pi1, ra1, rb1, rp1, si1, si1f, rz1)
     scatter_users_second(1, pu1, ra1, rb1, sa1, sb1, qa1, qb1)
-    scatter_items_second(1, pi1, rp1, si1, si1f, rz1)
     grad_users[...] = scatter_users_done(1, sa1, sb1, qa1, qb1)
     grad_items[...] = scatter_items_done(1, si1f, rz1)
 
@@ -382,26 +396,35 @@
     scatter_items_sent(1, rp1, rz1)
 
 
+def write_out(a, b, c, d, ah, bh, ch, dh, sem):
+    copies = [pltpu.make_async_copy(src, dst, sem.at[n]) for n, (src, dst) in enumerate(((a, ah), (b, bh), (c, ch), (d, dh)))]
+    for one in copies:
+        one.start()
+    for one in copies:
+        one.wait()
+
+
 def local(users, items, udeg, ideg, tiles, trows, tcols, tcount, bu, bp, bn):
     vmem = pl.BlockSpec(memory_space=pltpu.VMEM)
-    smem = pl.BlockSpec(memory_space=pltpu.SMEM)
-    hbm = pl.BlockSpec(memory_space=pl.ANY)
+    hbm = pl.BlockSpec(memory_space=pltpu.HBM)
     V = pltpu.VMEM
     order = (8, 128)
     fields = (NY, NX, UC, D)
     fieldi = (NZ, 2, IC, D)
+    out_shape = (
+        jax.ShapeDtypeStruct((UC, D), BF16),
+        jax.ShapeDtypeStruct((IC, D), BF16),
+        jax.ShapeDtypeStruct((UC, D), F32),
+        jax.ShapeDtypeStruct((IC, D), F32),
+    )
+    args = (users[0, 0], items[0, 0], udeg[0], ideg[0], tiles[0, 0], trows[0], tcols[0], tcount, bu[0], bp[0], bn[0])
     outs = pl.pallas_call(
         kernel,
-        out_shape=(
-            jax.ShapeDtypeStruct((UC, D), BF16),
-            jax.ShapeDtypeStruct((IC, D), BF16),
-            jax.ShapeDtypeStruct((UC, D), F32),
-            jax.ShapeDtypeStruct((IC, D), F32),
-        ),
-        in_specs=[vmem, vmem, vmem, vmem, hbm, vmem, vmem, smem, vmem, vmem, vmem],
+        out_shape=out_shape,
+        in_specs=[hbm] * 11,
         out_specs=(vmem,) * 4,
-        scratch_shapes=[
-            V((TILES, TB, TB), BF16),
+        scratch_shapes=[V(a.shape, a.dtype) for a in args]
+        + [
             V((TILES, TB, TB), BF16),
             V(order, I32),
             V(order, I32),
@@ -421,10 +444,10 @@
             V(fields, BF16),
             V(fieldi, F32),
             V(fieldi, F32),
-            V((NY - 1, NX, HU, D), F32),
-            V((NX - 1, NY, HU, D), F32),
-            V((NY - 1, NX, HU, D), BF16),
-            V((NX - 1, NY, HU, D), BF16),
+            V((NX // 2, NY - 1, 2, HU, D), F32),
+            V((NY // 2, NX - 1, 2, HU, D), F32),
+            V((NX // 2, NY - 1, 2, HU, D), BF16),
+            V((NY // 2, NX - 1, 2, HU, D), BF16),
             V((NX, HU, D), F32),
             V((NY, HU, D), F32),
             V((NX, HU, D), F32),
@@ -440,19 +463,30 @@
             V((IC, D), F32),
             V((NZ - 1, IC, D), F32),
             V((NZ - 1, IC, D), BF16),
-            SEM,
+            SEM((13,)),
             SEM((2, 11)),
+            SEM((2, NX - 1)),
+            SEM((2, NY - 1)),
             SEM((2, NZ - 1)),
             SEM((2, 11)),
+            SEM((2, NX // 2)),
+            SEM((2, NY // 2)),
             SEM((2, NZ)),
         ],
         compiler_params=pltpu.CompilerParams(
-            collective_id=0, has_side_effects=True, vmem_limit_bytes=48 * 1024 * 1024
+            collective_id=0, has_side_effects=True, vmem_limit_bytes=60 * 1024 * 1024
         ),
         name="lightgcn",
-    )(
-        users[0, 0], items[0, 0], udeg[0], ideg[0], tiles[0, 0], trows[0], tcols[0], tcount, bu[0], bp[0], bn[0]
-    )
+    )(*args)
+    outs = pl.pallas_call(
+        write_out,
+        out_shape=out_shape,
+        in_specs=[hbm] * 4,
+        out_specs=(hbm,) * 4,
+        scratch_shapes=[SEM((4,))],
+        compiler_params=pltpu.CompilerParams(vmem_limit_bytes=60 * 1024 * 1024),
+        name="write_out",
+    )(*outs)
     return tuple(o[None, None] for o in outs)
 
 

time: 106 us -> 81.4 us (0.77)
  Pallas kernels: 94.4 us -> 79.9 us
  local copies, waits for them, and re-layouts: 9.96 us -> 0 us
    pallas_call x1 -> x2, Pallas kernels: 94.4 us -> 79.9 us  [the longest x1 75.1 us: local(): pl.pallas_call(kernel, out_shape=out_shape, in_specs=[hbm] * 11, out_spec...]
    unnamed x24 -> x0, local copies, waits for them, and re-layouts: 9.96 us -> none
where the time goes in v2:
time: 81.4 us; the launch traced here: 81.2 us
  Pallas kernels  79.9 us (98%)
  between operations  1.29 us (2%)
    pallas_call x1, Pallas kernels, local(): pl.pallas_call(kernel, out_shape=out_shape, in_specs=[hbm] * 11, out_spec...  75.1 us
    pallas_call x1, Pallas kernels, local(): pl.pallas_call(write_out, out_shape=out_shape, in_specs=[hbm] * 4, out_sp...  4.86 us

profile of v2, /device:TPU:1, one launch (start us, length us, event | category | flops | bytes accessed | tf_op | source)
XLA Modules:
  0.0 81.2 jit_solution(4122910669727231599)
XLA Ops:
  1.3 75.1 %lightgcn.1 = (bf16[32,128]{1,0:T(8,128)(2,1)}, bf16[128,128]{1,0:T(8,128)(2,1)}, f32[32,128]{1,0:T(8,128)}, f32[128,128]{1,0:T(8,128)}) custom-call(bf16[32,128]{1,0:T(8,128)(2,1)} %bitcast.16, bf16[128,128]{1,0:T(8,128)(2,1)} %bitcast.15, s32[1,32]{1,0:T(1,128)} %bitcast.20, s32[1,128]{1,0:T(1,128)} %bitcast.21, bf16[48,128,128]{2,1,0:T(8,128)(2,1)} %bitcast.14, ...), custom_call_target="tpu_custom_call" | custom-call | tf_op jit(solution)/shard_map/lightgcn/pallas_call | solution.py:421
  76.4 4.9 %write_out.1 = (bf16[32,128]{1,0:T(8,128)(2,1)}, bf16[128,128]{1,0:T(8,128)(2,1)}, f32[32,128]{1,0:T(8,128)}, f32[128,128]{1,0:T(8,128)}) custom-call(bf16[32,128]{1,0:T(8,128)(2,1)} %get-tuple-element.12.a, bf16[128,128]{1,0:T(8,128)(2,1)} %get-tuple-element.13.b, f32[32,128]{1,0:T(8,128)} %get-tuple-element.14.c, f32[128,128]{1,0:T(8,128)} %get-tuple-element.15.d), custom_call_target="tpu_custom_call" | custom-call | tf_op jit(solution)/shard_map/write_out/pallas_call | solution.py:481

commit v3 on v2

--- a/solution.py
+++ b/solution.py
@@ -21,6 +21,7 @@
 NEAR_FIRST = (0, 6, 1, 5, 2, 4, 3)
 FAR_FIRST = (2, 1, 3, 0)
 UNROLL = 16
+ORDER_OUT = (3, 1, 2, 0)
 
 SEM = pltpu.SemaphoreType.DMA
 
@@ -76,6 +77,7 @@
 
 def kernel(
     users_h, items_h, udeg_h, ideg_h, tiles_h, trows_h, tcols_h, tcount_h, bu_h, bp_h, bn_h,
+    user_out_h, item_out_h, grad_users_h, grad_items_h,
     user_out, item_out, grad_users, grad_items,
     users, items, udeg, ideg, tv, trows, tcols, tcount, bu, bp, bn,
     tt, ordr_v, ordc_v, ordr, ordc, part,
@@ -127,10 +129,8 @@
     def greet(device):
         pl.semaphore_signal(barrier, inc=1, device_id=device, device_id_type=MESH)
 
+    each_far_first(NX - 1, lambda k: [greet(at_x(k + 1)[1]), greet(at_y(k + 1)[1]), greet(at_z(k + 1)[1])])
     greet(partner)
-    each(NX - 1, lambda k: greet(at_x(k + 1)[1]))
-    each(NY - 1, lambda k: greet(at_y(k + 1)[1]))
-    each(NZ - 1, lambda k: greet(at_z(k + 1)[1]))
 
     for n in range(4):
         loads[n].wait()
@@ -138,20 +138,22 @@
     di = inv_sqrt(column(ideg[...], IC).astype(F32))
 
     def gather_start(q, uf, itf, user_val, item_val):
-        uf[y, x] = (user_val * du).astype(BF16)
-        itf[z, core] = (item_val * di).astype(BF16)
-        if q == 0:
-            pl.semaphore_wait(barrier, NX + NY + NZ - 2)
         s = ag_sem.at[q]
         mine_u = uf.at[y, x]
         mine_i = itf.at[z, core]
+        itf[z, core] = (item_val() * di).astype(BF16)
+        if q == 0:
+            uf[y, x] = (user_val() * du).astype(BF16)
+            pl.semaphore_wait(barrier, NX + NY + NZ - 2)
+        each_far_first(NZ - 1, lambda k: send(mine_i, mine_i, s.at[0], ag_zs.at[q, k], at_z(k + 1)[1]))
+        if q == 1:
+            uf[y, x] = (user_val() * du).astype(BF16)
 
         def one(k):
             send(mine_u, mine_u, s.at[3], ag_xs.at[q, k], at_x(k + 1)[1])
             send(mine_u, mine_u, s.at[5], ag_ys.at[q, k], at_y(k + 1)[1])
 
         each_far_first(NX - 1, one)
-        each_far_first(NZ - 1, lambda k: send(mine_i, mine_i, s.at[0], ag_zs.at[q, k], at_z(k + 1)[1]))
         send(mine_i, mine_i, s.at[1], s.at[2], partner)
 
     def gather_second(q, uf):
@@ -329,7 +331,7 @@
         scatter_items_first(q, pi, rp)
         scatter_items_second(q, pi, rp, si, keep, rz)
 
-    gather_start(0, uf0, itf0, users[...].astype(F32), items[...].astype(F32))
+    gather_start(0, uf0, itf0, lambda: users[...].astype(F32), lambda: items[...].astype(F32))
     for n in range(5, 8):
         loads[n].wait()
     live = lax.broadcasted_iota(I32, (1, TILES), 1) < jnp.broadcast_to(tcount[...], (1, TILES))
@@ -364,6 +366,14 @@
     i_out = scatter_items_done(0, si0.at[z], rz0).astype(BF16)
     user_out[...] = u_out
     item_out[...] = i_out
+    stores = [
+        pltpu.make_async_copy(src, dst, load_sem.at[13 + n])
+        for n, (src, dst) in enumerate(
+            ((user_out, user_out_h), (item_out, item_out_h), (grad_users, grad_users_h), (grad_items, grad_items_h))
+        )
+    ]
+    stores[0].start()
+    stores[1].start()
 
     upad[0:UC] = u_out
     upad[UC:IC] = jnp.zeros((IC - UC, D), BF16)
@@ -377,16 +387,17 @@
         lo = (v - hi.astype(F32)).astype(BF16)
         return jnp.dot(hotT, hi, preferred_element_type=F32) + jnp.dot(hotT, lo, preferred_element_type=F32)
 
-    g_u = spread(huT[...], weight * d_vec)
-    g_i = spread(hdT[...], weight * u_vec)
-
-    gather_start(1, uf1, itf1, g_u, g_i)
+    gather_start(
+        1, uf1, itf1, lambda: spread(huT[...], weight * d_vec), lambda: spread(hdT[...], weight * u_vec)
+    )
     gather_second(1, uf1)
     gather_forward(1, itf1)
     products(1, uf1, itf1, pu1, pi1, ra1, rb1, rp1, si1, si1f, rz1)
     scatter_users_second(1, pu1, ra1, rb1, sa1, sb1, qa1, qb1)
+    grad_items[...] = scatter_items_done(1, si1f, rz1)
+    stores[3].start()
     grad_users[...] = scatter_users_done(1, sa1, sb1, qa1, qb1)
-    grad_items[...] = scatter_items_done(1, si1f, rz1)
+    stores[2].start()
 
     gather_sent(0, uf0, itf0)
     gather_sent(1, uf1, itf1)
@@ -394,18 +405,24 @@
     scatter_users_sent(1, ra1, rb1, qa1, qb1)
     scatter_items_sent(0, rp0, rz0)
     scatter_items_sent(1, rp1, rz1)
-
-
-def write_out(a, b, c, d, ah, bh, ch, dh, sem):
-    copies = [pltpu.make_async_copy(src, dst, sem.at[n]) for n, (src, dst) in enumerate(((a, ah), (b, bh), (c, ch), (d, dh)))]
-    for one in copies:
-        one.start()
-    for one in copies:
+    for one in stores:
         one.wait()
 
 
+def write_out(a, b, c, d, ah, bh, ch, dh, av, bv, cv, dv, sem):
+    triples = ((a, av, ah), (b, bv, bh), (c, cv, ch), (d, dv, dh))
+    reads = [pltpu.make_async_copy(src, mid, sem.at[n]) for n, (src, mid, _) in enumerate(triples)]
+    writes = [pltpu.make_async_copy(mid, dst, sem.at[n + 4]) for n, (_, mid, dst) in enumerate(triples)]
+    for n in ORDER_OUT:
+        reads[n].start()
+    for n in ORDER_OUT:
+        reads[n].wait()
+        writes[n].start()
+    for n in ORDER_OUT:
+        writes[n].wait()
+
+
 def local(users, items, udeg, ideg, tiles, trows, tcols, tcount, bu, bp, bn):
-    vmem = pl.BlockSpec(memory_space=pltpu.VMEM)
     hbm = pl.BlockSpec(memory_space=pltpu.HBM)
     V = pltpu.VMEM
     order = (8, 128)
@@ -422,8 +439,9 @@
         kernel,
         out_shape=out_shape,
         in_specs=[hbm] * 11,
-        out_specs=(vmem,) * 4,
-        scratch_shapes=[V(a.shape, a.dtype) for a in args]
+        out_specs=(hbm,) * 4,
+        scratch_shapes=[V(o.shape, o.dtype) for o in out_shape]
+        + [V(a.shape, a.dtype) for a in args]
         + [
             V((TILES, TB, TB), BF16),
             V(order, I32),
@@ -463,7 +481,7 @@
             V((IC, D), F32),
             V((NZ - 1, IC, D), F32),
             V((NZ - 1, IC, D), BF16),
-            SEM((13,)),
+            SEM((17,)),
             SEM((2, 11)),
             SEM((2, NX - 1)),
             SEM((2, NY - 1)),
@@ -483,7 +501,7 @@
         out_shape=out_shape,
         in_specs=[hbm] * 4,
         out_specs=(hbm,) * 4,
-        scratch_shapes=[SEM((4,))],
+        scratch_shapes=[V(o.shape, o.dtype) for o in out_shape] + [SEM((8,))],
         compiler_params=pltpu.CompilerParams(vmem_limit_bytes=60 * 1024 * 1024),
         name="write_out",
     )(*outs)

time: 81.4 us -> 77.8 us (0.956)
  Pallas kernels: 79.9 us -> 76.3 us
    pallas_call x1, Pallas kernels: 4.86 us -> 1.55 us  [local(): pl.pallas_call(write_out, out_shape=out_shape, in_specs=[hbm] * 4, out_sp...]
where the time goes in v3:
time: 77.8 us; the launch traced here: 77.6 us
  Pallas kernels  76.3 us (98%)
  between operations  1.29 us (2%)
    pallas_call x1, Pallas kernels, local(): pl.pallas_call(kernel, out_shape=out_shape, in_specs=[hbm] * 11, out_spec...  74.8 us

profile of v3, /device:TPU:1, one launch (start us, length us, event | category | flops | bytes accessed | tf_op | source)
XLA Modules:
  0.0 77.6 jit_solution(13933709970957638098)
XLA Ops:
  1.3 74.8 %lightgcn.1 = (bf16[32,128]{1,0:T(8,128)(2,1)}, bf16[128,128]{1,0:T(8,128)(2,1)}, f32[32,128]{1,0:T(8,128)}, f32[128,128]{1,0:T(8,128)}) custom-call(bf16[32,128]{1,0:T(8,128)(2,1)} %bitcast.16, bf16[128,128]{1,0:T(8,128)(2,1)} %bitcast.15, s32[1,32]{1,0:T(1,128)} %bitcast.20, s32[1,128]{1,0:T(1,128)} %bitcast.21, bf16[48,128,128]{2,1,0:T(8,128)(2,1)} %bitcast.14, ...), custom_call_target="tpu_custom_call" | custom-call | tf_op jit(solution)/shard_map/lightgcn/pallas_call | solution.py:438
  76.1 1.6 %write_out.1 = (bf16[32,128]{1,0:T(8,128)(2,1)}, bf16[128,128]{1,0:T(8,128)(2,1)}, f32[32,128]{1,0:T(8,128)}, f32[128,128]{1,0:T(8,128)}) custom-call(bf16[32,128]{1,0:T(8,128)(2,1)} %get-tuple-element.12.a, bf16[128,128]{1,0:T(8,128)(2,1)} %get-tuple-element.13.b, f32[32,128]{1,0:T(8,128)} %get-tuple-element.14.c, f32[128,128]{1,0:T(8,128)} %get-tuple-element.15.d), custom_call_target="tpu_custom_call" | custom-call | tf_op jit(solution)/shard_map/write_out/pallas_call | solution.py:499
